TPU v7x, 32 devices: a whole 2x2x4 slice. The times are simulated.
32 devices in a mesh: ctx: 8 (over y, x, core), tp: 4 (over z).
Axes of the slice: x: 2, y: 2, z: 4, core: 2. Of those that a mesh axis runs over, the one named last changes fastest.
Arguments:
- tokens: bfloat16 [8, 1024, 768], P(None, 'ctx'), may hold values from -6 to 6
- cotangent: bfloat16 [8, 1024, 768], P(None, 'ctx'), may hold values from -1.5 to 1.5
- seq_lengths: int32 [8], replicated, may hold values from 256 to 1024, as said below
- combined_weight: bfloat16 [2, 768, 12, 3, 64], P(None, None, 'tp'), may hold values from -0.21875 to 0.21875
- joined_bias: bfloat16 [2, 12, 2, 64], P(None, 'tp'), may hold values from -3 to 3
- attention_out_weight: bfloat16 [2, 768, 768], P(None, 'tp'), may hold values from -9 to 9
- attention_out_bias: bfloat16 [2, 768], replicated, may hold values from -3 to 3
- expand_weight: bfloat16 [2, 768, 3072], P(None, None, 'tp'), may hold values from -0.21875 to 0.21875
- expand_bias: bfloat16 [2, 3072], P(None, 'tp'), may hold values from -3 to 3
- contract_weight: bfloat16 [2, 3072, 768], P(None, 'tp'), may hold values from -0.109375 to 0.109375
- contract_bias: bfloat16 [2, 768], replicated, may hold values from -3 to 3
- norm_gains: bfloat16 [2, 2, 768], replicated, may hold values from 0.25 to 1.75
- norm_shifts: bfloat16 [2, 2, 768], replicated, may hold values from -3 to 3
Outputs:
- outputs: float32 [8, 1024, 768], P(None, 'ctx')
- tokens_grad: float32 [8, 1024, 768], P(None, 'ctx')
- grad_joined: float32 [2, 768, 12, 3, 64], P(None, None, 'tp')
- grad_qvbias: float32 [2, 12, 2, 64], P(None, 'tp')
- grad_mixer: float32 [2, 768, 768], P(None, 'tp')
- grad_mbias: float32 [2, 768], replicated
- grad_upward: float32 [2, 768, 3072], P(None, None, 'tp')
- grad_ubias: float32 [2, 3072], P(None, 'tp')
- grad_down: float32 [2, 3072, 768], P(None, 'tp')
- grad_dbias: float32 [2, 768], replicated
- grad_gains: float32 [2, 2, 768], replicated
- grad_shifts: float32 [2, 2, 768], replicated
Inputs may be any that keep to these rules, and one draw needn't show every extreme that they name: `seq_lengths`: at least one sequence has length 1024 in every draw.
All inputs are finite; a program needn't handle non-finite values.
Results may differ from a plain program's by a relative error of at most 0.018.
Values may be sent and summed in bfloat16 or wider, within the bound.
A program may use at most 448 MiB of HBM per device.

v0:
```python
import jax
import jax.numpy as jnp
from jax import lax
from jax.sharding import PartitionSpec as P

EPS = 1e-12
MASKED = -1e30


def normalize(resid, norm_gain, norm_shift):
    row_mean = jnp.mean(resid, axis=-1, keepdims=True)
    centred = resid - row_mean
    spread = jnp.mean(centred * centred, axis=-1, keepdims=True)
    return centred * lax.rsqrt(spread + EPS) * norm_gain + norm_shift


def smooth_gate(value):
    return (
        0.5
        * value
        * (1.0 + jnp.tanh(0.7978845608028654 * (value + 0.044715 * value * value * value)))
    )


def attention_scores(queries, key_rows, key_valid, scale):
    scores = (
        jnp.einsum("sqhd,skhd->shqk", queries, key_rows, preferred_element_type=jnp.float32) * scale
    )
    return jnp.where(key_valid[:, None, None, :], scores, MASKED)


def share_sum(partial_rows):
    return lax.psum_scatter(partial_rows, "tp", scatter_dimension=1, tiled=True)


def share_gather(rows_low):
    return lax.all_gather(rows_low, "tp", axis=1, tiled=True)


def take_share(full_rows):
    share_rows = full_rows.shape[1] // lax.axis_size("tp")
    return lax.dynamic_slice_in_dim(full_rows, lax.axis_index("tp") * share_rows, share_rows, 1)


def forward_layer(
    hidden,
    hidden_reduced,
    seq_lengths,
    combined_weight,
    joined_bias,
    attention_out_weight,
    attention_out_bias,
    expand_weight,
    expand_bias,
    contract_weight,
    contract_bias,
    norm_gains,
    norm_shifts,
):
    n_seqs, n_rows, width = hidden_reduced.shape
    n_heads = combined_weight.shape[1]
    head_dim = combined_weight.shape[3]
    scale = head_dim ** (-0.5)
    joined_flat = combined_weight.reshape(width, -1)
    combined_projected = jnp.einsum(
        "sbd,dc->sbc", hidden_reduced, joined_flat, preferred_element_type=jnp.float32
    )
    combined_projected = combined_projected.reshape(n_seqs, n_rows, n_heads, 3, head_dim)
    queries = (combined_projected[..., 0, :] + joined_bias[:, 0, :]).astype(jnp.bfloat16)
    key_rows = combined_projected[..., 1, :].astype(jnp.bfloat16)
    value_rows = (combined_projected[..., 2, :] + joined_bias[:, 1, :]).astype(jnp.bfloat16)
    all_keys, all_values = (
        lax.all_gather(key_rows.reshape(n_seqs, n_rows, -1), "ctx", axis=1, tiled=True),
        lax.all_gather(value_rows.reshape(n_seqs, n_rows, -1), "ctx", axis=1, tiled=True),
    )
    total_len = all_keys.shape[1]
    all_keys = all_keys.reshape(n_seqs, total_len, n_heads, head_dim)
    all_values = all_values.reshape(n_seqs, total_len, n_heads, head_dim)
    key_valid = jnp.arange(total_len)[None, :] < seq_lengths[:, None]
    scores = attention_scores(queries, all_keys, key_valid, scale)
    row_max = jnp.max(scores, axis=-1, keepdims=True)
    log_total = row_max + jnp.log(jnp.sum(jnp.exp(scores - row_max), axis=-1, keepdims=True))
    attn_probs = jnp.exp(scores - log_total).astype(jnp.bfloat16)
    merged_head_output = jnp.einsum(
        "shqk,skhd->sqhd", attn_probs, all_values, preferred_element_type=jnp.float32
    )
    merged_head_output = merged_head_output.astype(jnp.bfloat16).reshape(n_seqs, n_rows, -1)
    attention_branch = jnp.einsum(
        "sbc,cd->sbd", merged_head_output, attention_out_weight, preferred_element_type=jnp.float32
    )
    attention_branch = share_sum(attention_branch)
    normalized_rows, first_back = jax.vjp(
        normalize, hidden + attention_branch + attention_out_bias, norm_gains[0], norm_shifts[0]
    )
    normed_low = normalized_rows.astype(jnp.bfloat16)
    normed_low = share_gather(normed_low)
    before_activation = (
        jnp.einsum("sbd,df->sbf", normed_low, expand_weight, preferred_element_type=jnp.float32)
        + expand_bias
    )
    activated_hidden, gate_back = jax.vjp(smooth_gate, before_activation)
    gated_low = activated_hidden.astype(jnp.bfloat16)
    feedforward_branch = jnp.einsum(
        "sbf,fd->sbd", gated_low, contract_weight, preferred_element_type=jnp.float32
    )
    feedforward_branch = share_sum(feedforward_branch)
    result, second_back = jax.vjp(
        normalize,
        normalized_rows + feedforward_branch + contract_bias,
        norm_gains[1],
        norm_shifts[1],
    )
    kept = (
        hidden_reduced,
        queries,
        key_rows,
        value_rows,
        all_keys,
        all_values,
        key_valid,
        log_total,
        merged_head_output,
        normed_low,
        gated_low,
        first_back,
        gate_back,
        second_back,
    )
    return (result, kept)


def backward_layer(
    grad_out, kept, combined_weight, attention_out_weight, expand_weight, contract_weight
):
    (
        hidden_reduced,
        queries,
        key_rows,
        value_rows,
        all_keys,
        all_values,
        key_valid,
        log_total,
        merged_head_output,
        normed_low,
        gated_low,
        first_back,
        gate_back,
        second_back,
    ) = kept
    n_seqs, n_rows, n_heads, head_dim = queries.shape
    width = hidden_reduced.shape[2]
    total_len = all_keys.shape[1]
    scale = head_dim ** (-0.5)
    d_resid_two, d_gain_two, d_shift_two = second_back(grad_out)
    d_down_bias = jnp.sum(d_resid_two, axis=(0, 1))
    d_branch_two = d_resid_two.astype(jnp.bfloat16)
    d_branch_two = share_gather(d_branch_two)
    d_down = jnp.einsum("sbf,sbd->fd", gated_low, d_branch_two, preferred_element_type=jnp.float32)
    d_gated = jnp.einsum(
        "sbd,fd->sbf", d_branch_two, contract_weight, preferred_element_type=jnp.float32
    )
    d_pre_gate = gate_back(d_gated)[0].astype(jnp.bfloat16)
    d_up_bias = jnp.sum(d_pre_gate.astype(jnp.float32), axis=(0, 1))
    d_upward = jnp.einsum("sbd,sbf->df", normed_low, d_pre_gate, preferred_element_type=jnp.float32)
    d_normed = jnp.einsum(
        "sbf,df->sbd", d_pre_gate, expand_weight, preferred_element_type=jnp.float32
    )
    d_normed = share_sum(d_normed) + d_resid_two
    d_resid_one, d_gain_one, d_shift_one = first_back(d_normed)
    d_mixer_bias = jnp.sum(d_resid_one, axis=(0, 1))
    d_branch = d_resid_one.astype(jnp.bfloat16)
    d_branch = share_gather(d_branch)
    d_mixer = jnp.einsum(
        "sbc,sbd->cd", merged_head_output, d_branch, preferred_element_type=jnp.float32
    )
    d_mixed = jnp.einsum(
        "sbd,cd->sbc", d_branch, attention_out_weight, preferred_element_type=jnp.float32
    )
    d_mixed = d_mixed.astype(jnp.bfloat16).reshape(n_seqs, n_rows, n_heads, head_dim)
    scores = attention_scores(queries, all_keys, key_valid, scale)
    probs_full = jnp.exp(scores - log_total)
    d_probs = jnp.einsum("sqhd,skhd->shqk", d_mixed, all_values, preferred_element_type=jnp.float32)
    row_delta = jnp.sum(probs_full * d_probs, axis=-1, keepdims=True)
    d_scores = (probs_full * (d_probs - row_delta)).astype(jnp.bfloat16)
    d_queries = (
        jnp.einsum("shqk,skhd->sqhd", d_scores, all_keys, preferred_element_type=jnp.float32)
        * scale
    )
    d_queries = d_queries.astype(jnp.bfloat16)
    key_part = (
        jnp.einsum("shqk,sqhd->skhd", d_scores, queries, preferred_element_type=jnp.float32) * scale
    )
    value_part = jnp.einsum(
        "shqk,sqhd->skhd",
        probs_full.astype(jnp.bfloat16),
        d_mixed,
        preferred_element_type=jnp.float32,
    )
    d_keys, d_values = (
        lax.psum_scatter(
            key_part.reshape(n_seqs, total_len, -1), "ctx", scatter_dimension=1, tiled=True
        ),
        lax.psum_scatter(
            value_part.reshape(n_seqs, total_len, -1), "ctx", scatter_dimension=1, tiled=True
        ),
    )
    d_keys = d_keys.reshape(n_seqs, n_rows, n_heads, head_dim)
    d_values = d_values.reshape(n_seqs, n_rows, n_heads, head_dim)
    d_keys = d_keys.astype(jnp.bfloat16)
    d_values = d_values.astype(jnp.bfloat16)
    d_joined_bias = jnp.stack(
        [
            jnp.sum(d_queries.astype(jnp.float32), axis=(0, 1)),
            jnp.sum(d_values.astype(jnp.float32), axis=(0, 1)),
        ],
        axis=1,
    )
    d_joined_out = jnp.stack([d_queries, d_keys, d_values], axis=3).reshape(n_seqs, n_rows, -1)
    d_joined = jnp.einsum(
        "sbd,sbc->dc", hidden_reduced, d_joined_out, preferred_element_type=jnp.float32
    )
    d_joined = d_joined.reshape(width, n_heads, 3, head_dim)
    d_hidden = jnp.einsum(
        "sbc,dc->sbd",
        d_joined_out,
        combined_weight.reshape(width, -1),
        preferred_element_type=jnp.float32,
    )
    d_hidden = share_sum(d_hidden) + d_resid_one
    small_grads = (
        d_mixer_bias,
        d_down_bias,
        jnp.stack([d_gain_one, d_gain_two]),
        jnp.stack([d_shift_one, d_shift_two]),
    )
    small_grads = lax.psum(
        (
            small_grads[0],
            small_grads[1],
            small_grads[2].astype(jnp.float32),
            small_grads[3].astype(jnp.float32),
        ),
        "tp",
    )
    grads = (
        d_joined,
        d_joined_bias,
        d_mixer,
        small_grads[0],
        d_upward,
        d_up_bias,
        d_down,
        small_grads[1],
        small_grads[2],
        small_grads[3],
    )
    return (d_hidden, grads)


def sum_layer(grads):
    return lax.psum(
        (
            grads[0],
            grads[1],
            grads[2],
            grads[3],
            grads[4],
            grads[5],
            grads[6],
            grads[7],
            grads[8],
            grads[9],
        ),
        "ctx",
    )


def on_device(
    tokens,
    cotangent,
    seq_lengths,
    combined_weight,
    joined_bias,
    attention_out_weight,
    attention_out_bias,
    expand_weight,
    expand_bias,
    contract_weight,
    contract_bias,
    norm_gains,
    norm_shifts,
):
    params = (
        combined_weight,
        joined_bias,
        attention_out_weight,
        attention_out_bias,
        expand_weight,
        expand_bias,
        contract_weight,
        contract_bias,
        norm_gains,
        norm_shifts,
    )
    n_layers = combined_weight.shape[0]
    hidden = tokens.astype(jnp.float32)
    hidden_reduced = tokens
    hidden = take_share(hidden)
    saved = []
    for layer_idx in range(n_layers):
        hidden, kept = forward_layer(
            hidden, hidden_reduced, seq_lengths, *[weight[layer_idx] for weight in params]
        )
        saved.append(kept)
        if layer_idx + 1 < n_layers:
            hidden_reduced = hidden.astype(jnp.bfloat16)
            hidden_reduced = share_gather(hidden_reduced)
    grad_now = cotangent.astype(jnp.float32)
    grad_now = take_share(grad_now)
    collected = []
    for layer_idx in reversed(range(n_layers)):
        grad_now, grads = backward_layer(
            grad_now,
            saved[layer_idx],
            combined_weight[layer_idx],
            attention_out_weight[layer_idx],
            expand_weight[layer_idx],
            contract_weight[layer_idx],
        )
        grads = sum_layer(grads)
        collected.insert(0, grads)
    stacked = tuple((jnp.stack([entry[member] for entry in collected]) for member in range(10)))
    hidden, grad_now = (
        lax.all_gather(hidden, "tp", axis=1, tiled=True),
        lax.all_gather(grad_now, "tp", axis=1, tiled=True),
    )
    return (
        hidden,
        grad_now,
        stacked[0],
        stacked[1],
        stacked[2],
        stacked[3],
        stacked[4],
        stacked[5],
        stacked[6],
        stacked[7],
        stacked[8],
        stacked[9],
    )


def solution(mesh):
    placed = (
        P(None, "ctx", None),
        P(None, "ctx", None),
        P(),
        P(None, None, "tp", None, None),
        P(None, "tp", None, None),
        P(None, "tp", None),
        P(),
        P(None, None, "tp"),
        P(None, "tp"),
        P(None, "tp", None),
        P(),
        P(),
        P(),
    )
    return jax.shard_map(
        on_device,
        mesh=mesh,
        in_specs=placed,
        out_specs=(
            P(None, "ctx", None),
            P(None, "ctx", None),
            P(None, None, "tp", None, None),
            P(None, "tp", None, None),
            P(None, "tp", None),
            P(),
            P(None, None, "tp"),
            P(None, "tp"),
            P(None, "tp", None),
            P(),
            P(),
            P(),
        ),
        check_vma=False,
    )
```

profile of v0, /device:TPU:0, one launch (start us, length us, event | category | flops | bytes accessed | tf_op | source)
XLA Modules:
  0.0 1609.7 jit_solution(18268180588646631589)
XLA Ops:
  12.3 34.3 %all-gather.16.cloned.1.call-done = bf16[8,1024,192]{1,2,0:T(8,128)(2,1)} async-done(((bf16[8,128,192]{1,2,0:T(8,128)(2,1)}), bf16[8,1024,192]{1,2,0:T(8,128)(2,1)}) %all-gather.16.cloned.1.call-update) | async-done | bytes 3145744 | tf_op jit(solution)/shard_map/all_gather | solution.py:73
  93.7 60.2 %reduce-scatter.13.cloned.1.call-done = f32[8,32,768]{2,1,0:T(8,128)} async-done(((f32[8,128,768]{2,1,0:T(8,128)}), f32[8,32,768]{2,1,0:T(8,128)}) %reduce-scatter.13.cloned.1.call-update) | async-done | bytes 786448 | tf_op jit(solution)/shard_map/reduce_scatter | solution.py:33
  156.7 37.2 %all-gather.18.cloned.1.call-done = bf16[8,128,768]{2,1,0:T(8,128)(2,1)} async-done(((bf16[8,32,768]{2,1,0:T(8,128)(2,1)}), bf16[8,128,768]{2,1,0:T(8,128)(2,1)}) %all-gather.18.cloned.1.call-update) | async-done | bytes 1572880 | tf_op jit(solution)/shard_map/all_gather | solution.py:37
  203.3 58.6 %reduce-scatter.15.cloned.1.call-done = f32[8,32,768]{2,1,0:T(8,128)} async-done(((f32[8,128,768]{2,1,0:T(8,128)}), f32[8,32,768]{2,1,0:T(8,128)}) %reduce-scatter.15.cloned.1.call-update) | async-done | bytes 786448 | tf_op jit(solution)/shard_map/reduce_scatter | solution.py:33
  265.2 36.7 %all-gather.20.cloned.1.call-done = bf16[8,128,768]{2,1,0:T(8,128)(2,1)} async-done(((bf16[8,32,768]{2,1,0:T(8,128)(2,1)}), bf16[8,128,768]{2,1,0:T(8,128)(2,1)}) %all-gather.20.cloned.1.call-update) | async-done | bytes 1572880 | tf_op jit(solution)/shard_map/all_gather | solution.py:37
  309.3 29.5 %all-gather.24.cloned.1.call-done = bf16[8,1024,192]{1,2,0:T(8,128)(2,1)} async-done(((bf16[8,128,192]{1,2,0:T(8,128)(2,1)}), bf16[8,1024,192]{1,2,0:T(8,128)(2,1)}) %all-gather.24.cloned.1.call-update) | async-done | bytes 3145744 | tf_op jit(solution)/shard_map/all_gather | solution.py:73
  384.9 60.3 %reduce-scatter.17.cloned.1.call-done = f32[8,32,768]{2,1,0:T(8,128)} async-done(((f32[8,128,768]{2,1,0:T(8,128)}), f32[8,32,768]{2,1,0:T(8,128)}) %reduce-scatter.17.cloned.1.call-update) | async-done | bytes 786448 | tf_op jit(solution)/shard_map/reduce_scatter | solution.py:33
  448.1 37.2 %all-gather.26.cloned.1.call-done = bf16[8,128,768]{2,1,0:T(8,128)(2,1)} async-done(((bf16[8,32,768]{2,1,0:T(8,128)(2,1)}), bf16[8,128,768]{2,1,0:T(8,128)(2,1)}) %all-gather.26.cloned.1.call-update) | async-done | bytes 1572880 | tf_op jit(solution)/shard_map/all_gather | solution.py:37
  494.3 59.1 %reduce-scatter.19.cloned.1.call-done = f32[8,32,768]{2,1,0:T(8,128)} async-done(((f32[8,128,768]{2,1,0:T(8,128)}), f32[8,32,768]{2,1,0:T(8,128)}) %reduce-scatter.19.cloned.1.call-update) | async-done | bytes 786448 | tf_op jit(solution)/shard_map/reduce_scatter | solution.py:33
  558.8 37.2 %all-gather.30.cloned.1.call-done = bf16[8,128,768]{2,1,0:T(8,128)(2,1)} async-done(((bf16[8,32,768]{2,1,0:T(8,128)(2,1)}), bf16[8,128,768]{2,1,0:T(8,128)(2,1)}) %all-gather.30.cloned.1.call-update) | async-done | bytes 1572880 | tf_op jit(solution)/shard_map/all_gather | solution.py:37
  607.4 59.2 %reduce-scatter.21.cloned.1.call-done = f32[8,32,768]{2,1,0:T(8,128)} async-done(((f32[8,128,768]{2,1,0:T(8,128)}), f32[8,32,768]{2,1,0:T(8,128)}) %reduce-scatter.21.cloned.1.call-update) | async-done | bytes 786448 | tf_op jit(solution)/shard_map/reduce_scatter | solution.py:33
  671.0 37.2 %all-gather.32.cloned.1.call-done = bf16[8,128,768]{2,1,0:T(8,128)(2,1)} async-done(((bf16[8,32,768]{2,1,0:T(8,128)(2,1)}), bf16[8,128,768]{2,1,0:T(8,128)(2,1)}) %all-gather.32.cloned.1.call-update) | async-done | bytes 1572880 | tf_op jit(solution)/shard_map/all_gather | solution.py:37
  752.1 29.3 %reduce-scatter.25.cloned.1.call-done = f32[8,128,192]{1,2,0:T(8,128)} async-done(((f32[8,1024,192]{1,2,0:T(8,128)}), f32[8,128,192]{1,2,0:T(8,128)}) %reduce-scatter.25.cloned.1.call-update) | async-done | bytes 786448 | tf_op jit(solution)/shard_map/reduce_scatter | solution.py:204
  783.3 63.5 %reduce-scatter.23.cloned.1.call-done = f32[8,128,192]{1,2,0:T(8,128)} async-done(((f32[8,1024,192]{1,2,0:T(8,128)}), f32[8,128,192]{1,2,0:T(8,128)}) %reduce-scatter.23.cloned.1.call-update) | async-done | bytes 786448 | tf_op jit(solution)/shard_map/reduce_scatter | solution.py:201
  852.5 60.3 %reduce-scatter.27.cloned.1.call-done = f32[8,32,768]{2,1,0:T(8,128)} async-done(((f32[8,128,768]{2,1,0:T(8,128)}), f32[8,32,768]{2,1,0:T(8,128)}) %reduce-scatter.27.cloned.1.call-update) | async-done | bytes 786448 | tf_op jit(solution)/shard_map/reduce_scatter | solution.py:33
  916.6 37.0 %all-gather.34.cloned.1.call-done = bf16[8,128,768]{2,1,0:T(8,128)(2,1)} async-done(((bf16[8,32,768]{2,1,0:T(8,128)(2,1)}), bf16[8,128,768]{2,1,0:T(8,128)(2,1)}) %all-gather.34.cloned.1.call-update) | async-done | bytes 1572880 | tf_op jit(solution)/shard_map/all_gather | solution.py:37
  964.9 59.2 %reduce-scatter.29.cloned.1.call-done = f32[8,32,768]{2,1,0:T(8,128)} async-done(((f32[8,128,768]{2,1,0:T(8,128)}), f32[8,32,768]{2,1,0:T(8,128)}) %reduce-scatter.29.cloned.1.call-update) | async-done | bytes 786448 | tf_op jit(solution)/shard_map/reduce_scatter | solution.py:33
  1029.1 37.2 %all-gather.36.cloned.1.call-done = bf16[8,128,768]{2,1,0:T(8,128)(2,1)} async-done(((bf16[8,32,768]{2,1,0:T(8,128)(2,1)}), bf16[8,128,768]{2,1,0:T(8,128)(2,1)}) %all-gather.36.cloned.1.call-update) | async-done | bytes 1572880 | tf_op jit(solution)/shard_map/all_gather | solution.py:37
  1110.1 29.3 %reduce-scatter.33.cloned.1.call-done = f32[8,128,192]{1,2,0:T(8,128)} async-done(((f32[8,1024,192]{1,2,0:T(8,128)}), f32[8,128,192]{1,2,0:T(8,128)}) %reduce-scatter.33.cloned.1.call-update) | async-done | bytes 786448 | tf_op jit(solution)/shard_map/reduce_scatter | solution.py:204
  1140.7 64.2 %reduce-scatter.31.cloned.1.call-done = f32[8,128,192]{1,2,0:T(8,128)} async-done(((f32[8,1024,192]{1,2,0:T(8,128)}), f32[8,128,192]{1,2,0:T(8,128)}) %reduce-scatter.31.cloned.1.call-update) | async-done | bytes 786448 | tf_op jit(solution)/shard_map/reduce_scatter | solution.py:201
  1232.4 37.5 %reduce-scatter.35.cloned.1.call-done = f32[8,32,768]{2,1,0:T(8,128)} async-done(((f32[8,128,768]{2,1,0:T(8,128)}), f32[8,32,768]{2,1,0:T(8,128)}) %reduce-scatter.35.cloned.1.call-update) | async-done | bytes 786448 | tf_op jit(solution)/shard_map/reduce_scatter | solution.py:33
  1272.2 62.7 %all-gather.28.cloned.1.call-done = f32[8,128,768]{2,1,0:T(8,128)} async-done(((f32[8,32,768]{2,1,0:T(8,128)}), f32[8,128,768]{2,1,0:T(8,128)}) %all-gather.28.cloned.1.call-update) | async-done | bytes 3145744 | tf_op jit(solution)/shard_map/all_gather | solution.py:335
  1381.2 151.4 %all-reduce.5.cloned.1.call-done = (f32[1,768,3,3,64]{1,4,3,2,0:T(8,128)}, f32[1,768,3,3,64]{1,4,3,2,0:T(8,128)}, f32[1,192,768]{2,1,0:T(8,128)}, f32[1,192,768]...) async-done(((f32[1,768,3,3,64]{1,4,3,2,0:T(8,128)}, f32[1,768,3,3,64]{1,4,3,2,0:T(8,128)}, ...) | async-done | bytes 14155792 | tf_op jit(solution)/shard_map/psum | solution.py:262
  1545.8 52.5 %all-gather.38.cloned.1.call-done = f32[8,128,768]{2,1,0:T(8,128)} async-done(((f32[8,32,768]{2,1,0:T(8,128)}), f32[8,128,768]{2,1,0:T(8,128)}) %all-gather.38.cloned.1.call-update) | async-done | bytes 3145744 | tf_op jit(solution)/shard_map/all_gather | solution.py:336
  (385 shorter events, 363.1 us)
Async XLA Ops:
  10.9 71.0 %all-gather.14.cloned.1.call-start = ((), (), s32[]{:S(2)}) async-start(), calls=%async_computation.12 | async-start | bytes 3538944 | tf_op jit(solution)/shard_map/all_gather | solution.py:74
  12.1 141.8 %reduce-scatter.13.cloned.1.call-start = ((), (), s32[]{:S(2)}) async-start(), calls=%async_computation.14 | async-start | bytes 3932160 | tf_op jit(solution)/shard_map/reduce_scatter | solution.py:33
  93.5 100.3 %all-gather.18.cloned.1.call-start = ((), (), s32[]{:S(2)}) async-start(), calls=%async_computation.15 | async-start | bytes 1966080 | tf_op jit(solution)/shard_map/all_gather | solution.py:37
  156.6 105.3 %reduce-scatter.15.cloned.1.call-start = ((), (), s32[]{:S(2)}) async-start(), calls=%async_computation.16 | async-start | bytes 3932160 | tf_op jit(solution)/shard_map/reduce_scatter | solution.py:33
  202.6 99.3 %all-gather.20.cloned.1.call-start = ((), (), s32[]{:S(2)}) async-start(), calls=%async_computation.17 | async-start | bytes 1966080 | tf_op jit(solution)/shard_map/all_gather | solution.py:37
  264.7 74.1 %all-gather.24.cloned.1.call-start = ((), (), s32[]{:S(2)}) async-start(), calls=%async_computation.19 | async-start | bytes 3538944 | tf_op jit(solution)/shard_map/all_gather | solution.py:73
  309.2 136.0 %reduce-scatter.17.cloned.1.call-start = ((), (), s32[]{:S(2)}) async-start(), calls=%async_computation.20 | async-start | bytes 3932160 | tf_op jit(solution)/shard_map/reduce_scatter | solution.py:33
  384.9 100.4 %all-gather.26.cloned.1.call-start = ((), (), s32[]{:S(2)}) async-start(), calls=%async_computation.21 | async-start | bytes 1966080 | tf_op jit(solution)/shard_map/all_gather | solution.py:37
  448.0 105.3 %reduce-scatter.19.cloned.1.call-start = ((), (), s32[]{:S(2)}) async-start(), calls=%async_computation.22 | async-start | bytes 3932160 | tf_op jit(solution)/shard_map/reduce_scatter | solution.py:33
  494.0 102.0 %all-gather.30.cloned.1.call-start = ((), (), s32[]{:S(2)}) async-start(), calls=%async_computation.24 | async-start | bytes 1966080 | tf_op jit(solution)/shard_map/all_gather | solution.py:37
  558.8 107.8 %reduce-scatter.21.cloned.1.call-start = ((), (), s32[]{:S(2)}) async-start(), calls=%async_computation.25 | async-start | bytes 3932160 | tf_op jit(solution)/shard_map/reduce_scatter | solution.py:33
  607.3 100.9 %all-gather.32.cloned.1.call-start = ((), (), s32[]{:S(2)}) async-start(), calls=%async_computation.26 | async-start | bytes 1966080 | tf_op jit(solution)/shard_map/all_gather | solution.py:37
  670.9 110.5 %reduce-scatter.25.cloned.1.call-start = ((), (), s32[]{:S(2)}) async-start(), calls=%async_computation.28 | async-start | bytes 7077888 | tf_op jit(solution)/shard_map/reduce_scatter | solution.py:204
  720.6 126.2 %reduce-scatter.23.cloned.1.call-start = ((), (), s32[]{:S(2)}) async-start(), calls=%async_computation.27 | async-start | bytes 7077888 | tf_op jit(solution)/shard_map/reduce_scatter | solution.py:201
  742.7 170.1 %reduce-scatter.27.cloned.1.call-start = ((), (), s32[]{:S(2)}) async-start(), calls=%async_computation.29 | async-start | bytes 3932160 | tf_op jit(solution)/shard_map/reduce_scatter | solution.py:33
  852.4 101.1 %all-gather.34.cloned.1.call-start = ((), (), s32[]{:S(2)}) async-start(), calls=%async_computation.30 | async-start | bytes 1966080 | tf_op jit(solution)/shard_map/all_gather | solution.py:37
  916.3 107.8 %reduce-scatter.29.cloned.1.call-start = ((), (), s32[]{:S(2)}) async-start(), calls=%async_computation.31 | async-start | bytes 3932160 | tf_op jit(solution)/shard_map/reduce_scatter | solution.py:33
  964.9 101.5 %all-gather.36.cloned.1.call-start = ((), (), s32[]{:S(2)}) async-start(), calls=%async_computation.32 | async-start | bytes 1966080 | tf_op jit(solution)/shard_map/all_gather | solution.py:37
  1029.1 110.4 %reduce-scatter.33.cloned.1.call-start = ((), (), s32[]{:S(2)}) async-start(), calls=%async_computation.34 | async-start | bytes 7077888 | tf_op jit(solution)/shard_map/reduce_scatter | solution.py:204
  1078.7 126.3 %reduce-scatter.31.cloned.1.call-start = ((), (), s32[]{:S(2)}) async-start(), calls=%async_computation.33 | async-start | bytes 7077888 | tf_op jit(solution)/shard_map/reduce_scatter | solution.py:201
  1103.1 166.8 %reduce-scatter.35.cloned.1.call-start = ((), (), s32[]{:S(2)}) async-start(), calls=%async_computation.35 | async-start | bytes 3932160 | tf_op jit(solution)/shard_map/reduce_scatter | solution.py:33
  1209.5 125.3 %all-gather.28.cloned.1.call-start = ((), (), s32[]{:S(2)}) async-start(), calls=%async_computation.23 | async-start | bytes 3932160 | tf_op jit(solution)/shard_map/all_gather | solution.py:335
  1210.1 322.5 %all-reduce.5.cloned.1.call-start = ((), (), s32[]{:S(2)}) async-start(), calls=%async_computation.37 | async-start | bytes 28311552 | tf_op jit(solution)/shard_map/psum | solution.py:262
  1232.4 366.0 %all-gather.38.cloned.1.call-start = ((), (), s32[]{:S(2)}) async-start(), calls=%async_computation.36 | async-start | bytes 3932160 | tf_op jit(solution)/shard_map/all_gather | solution.py:336
  (94 other events, 4079.8 us)
Sparse Core Ops, SparseCore 0:
  11.1 35.5 all-gather.15
  49.1 32.8 all-gather.13
  93.6 60.2 reduce-scatter.12
  156.7 37.1 all-gather.17
  202.7 59.1 reduce-scatter.14
  264.8 37.0 all-gather.19
  385.0 60.2 reduce-scatter.16
  448.1 37.1 all-gather.25
  494.2 59.1 reduce-scatter.18
  558.9 37.0 all-gather.29
  607.4 59.0 reduce-scatter.20
  671.1 37.1 all-gather.31
  720.7 60.6 reduce-scatter.24
  785.0 61.7 reduce-scatter.22
  852.6 60.2 reduce-scatter.26
  916.4 37.0 all-gather.33
  965.0 59.0 reduce-scatter.28
  1029.2 37.1 all-gather.35
  1078.8 60.6 reduce-scatter.32
  1143.2 61.7 reduce-scatter.30
  1209.6 60.2 reduce-scatter.34
  1271.4 63.4 all-gather.27
  1340.7 191.8 all-reduce.4
  1534.7 63.5 all-gather.37
  (2 shorter events, 64.4 us)
where the time goes:
time: 1620 us; the launch traced here: 1610 us
  waiting for transfers between devices  1290 us (80%)
  matrix products  162 us (10%)
  other arithmetic  73.8 us (5%)
  blocking collectives  42.2 us (3%)
  local copies, waits for them, and re-layouts  28.2 us (2%)
    reduce_scatter x8, waiting for transfers between devices, share_sum(): return lax.psum_scatter(partial_rows, 'tp', scatter_dimension=1, tiled=True)  454 us
    all_gather x7, waiting for transfers between devices, share_gather(): return lax.all_gather(rows_low, 'tp', axis=1, tiled=True)  260 us
    psum x1, waiting for transfers between devices, sum_layer(): lax.psum((grads[0], grads[1], grads[2], grads[3], grads[4], grads[5], gra...  151 us
    reduce_scatter x2, waiting for transfers between devices, backward_layer(): lax.psum_scatter(key_part.reshape(n_seqs, total_len, -1), 'ctx', scatter_...  128 us
    all_gather x2, waiting for transfers between devices, forward_layer(): lax.all_gather(key_rows.reshape(n_seqs, n_rows, -1), 'ctx', axis=1, tiled...  63.8 us
    all_gather x1, waiting for transfers between devices, on_device(): lax.all_gather(hidden, 'tp', axis=1, tiled=True)  62.7 us
    reduce_scatter x2, waiting for transfers between devices, backward_layer(): lax.psum_scatter(value_part.reshape(n_seqs, total_len, -1), 'ctx', scatte...  58.6 us
    all_gather x2, waiting for transfers between devices, forward_layer(): lax.all_gather(value_rows.reshape(n_seqs, n_rows, -1), 'ctx', axis=1, til...  53.5 us
  transfers between devices with their start and end apart: 26, of which 26 were waited for; matrix products, arithmetic and copies ran while one was open for 7% of the time, Pallas kernels for 0%

commit v1 on v0

--- a/solution.py
+++ b/solution.py
@@ -350,6 +350,261 @@
         stacked[9],
     )
 
+def rows_of(array, axis_name, dim):
+    share = array.shape[dim] // lax.axis_size(axis_name)
+    return lax.dynamic_slice_in_dim(array, lax.axis_index(axis_name) * share, share, dim)
+
+
+def after(value, *earlier):
+    return lax.optimization_barrier((value,) + earlier)[0]
+
+
+def fetch_columns(weight):
+    part = lax.all_gather(rows_of(weight, "ctx", 0), "tp", axis=0)
+    part = part.transpose(1, 0, 2).reshape(part.shape[1], -1)
+    return lax.all_gather(part, "ctx", axis=0, tiled=True)
+
+
+def fetch_rows(weight):
+    part = lax.all_gather(rows_of(weight, "ctx", 0), "tp", axis=0)
+    whole = lax.all_gather(part, "ctx", axis=1, tiled=True)
+    return whole.reshape(-1, whole.shape[2])
+
+
+def reduce_columns(grad):
+    n_tp = lax.axis_size("tp")
+    part = lax.psum_scatter(grad.astype(jnp.bfloat16), "ctx", scatter_dimension=0, tiled=True)
+    part = part.reshape(part.shape[0], n_tp, -1).transpose(1, 0, 2)
+    return lax.psum_scatter(part, "tp", scatter_dimension=0)
+
+
+def reduce_rows(grad):
+    n_tp = lax.axis_size("tp")
+    part = grad.astype(jnp.bfloat16).reshape(n_tp, -1, grad.shape[1])
+    part = lax.psum_scatter(part, "ctx", scatter_dimension=1, tiled=True)
+    return lax.psum_scatter(part, "tp", scatter_dimension=0)
+
+
+def spread(part):
+    return lax.all_gather(part, "ctx", axis=0, tiled=True).astype(jnp.float32)
+
+
+def to_heads(rows, n_groups):
+    n_rows = rows.shape[0] * n_groups // lax.axis_size("ctx")
+    blocks = rows.reshape(-1, n_rows, n_groups, rows.shape[1] // n_groups)
+    blocks = blocks.transpose(0, 2, 1, 3).reshape(-1, n_rows, blocks.shape[3])
+    blocks = lax.all_to_all(blocks, "ctx", 0, 0, tiled=True)
+    return blocks.reshape(-1, blocks.shape[2])
+
+
+def to_rows(whole, n_groups):
+    n_ctx = lax.axis_size("ctx")
+    blocks = whole.reshape(n_ctx, whole.shape[0] // n_ctx, whole.shape[1])
+    blocks = lax.all_to_all(blocks, "ctx", 0, 0, tiled=True)
+    blocks = blocks.reshape(n_ctx // n_groups, n_groups, blocks.shape[1], blocks.shape[2])
+    blocks = blocks.transpose(0, 2, 1, 3)
+    return blocks.reshape(-1, n_groups * whole.shape[1])
+
+
+def matmul(left, right):
+    return jnp.dot(left, right, preferred_element_type=jnp.float32)
+
+
+def matmul_tn(left, right):
+    return lax.dot_general(left, right, (((0,), (0,)), ((), ())), preferred_element_type=jnp.float32)
+
+
+def matmul_nt(left, right):
+    return lax.dot_general(left, right, (((1,), (1,)), ((), ())), preferred_element_type=jnp.float32)
+
+
+def attend(joined, key_valid, head_dim):
+    total_len = joined.shape[0]
+    scale = head_dim ** (-0.5)
+    parts = joined.reshape(total_len, -1, 3, head_dim).transpose(2, 1, 0, 3)
+    queries, keys, values = parts[0], parts[1], parts[2]
+    scores = jnp.einsum("hqd,hkd->hqk", queries, keys, preferred_element_type=jnp.float32) * scale
+    scores = jnp.where(key_valid[None, None, :], scores, MASKED)
+    row_max = jnp.max(scores, axis=-1, keepdims=True)
+    log_total = row_max + jnp.log(jnp.sum(jnp.exp(scores - row_max), axis=-1, keepdims=True))
+    probs = jnp.exp(scores - log_total).astype(jnp.bfloat16)
+    mixed = jnp.einsum("hqk,hkd->hqd", probs, values, preferred_element_type=jnp.float32)
+    mixed = mixed.astype(jnp.bfloat16).transpose(1, 0, 2).reshape(total_len, -1)
+    return mixed, (queries, keys, values, log_total)
+
+
+def attend_back(d_mixed, kept, key_valid):
+    queries, keys, values, log_total = kept
+    n_heads, total_len, head_dim = queries.shape
+    scale = head_dim ** (-0.5)
+    d_mixed = d_mixed.reshape(total_len, n_heads, head_dim).transpose(1, 0, 2)
+    scores = jnp.einsum("hqd,hkd->hqk", queries, keys, preferred_element_type=jnp.float32) * scale
+    scores = jnp.where(key_valid[None, None, :], scores, MASKED)
+    probs = jnp.exp(scores - log_total)
+    d_probs = jnp.einsum("hqd,hkd->hqk", d_mixed, values, preferred_element_type=jnp.float32)
+    row_delta = jnp.sum(probs * d_probs, axis=-1, keepdims=True)
+    d_scores = (probs * (d_probs - row_delta)).astype(jnp.bfloat16)
+    probs = probs.astype(jnp.bfloat16)
+    d_queries = jnp.einsum("hqk,hkd->hqd", d_scores, keys, preferred_element_type=jnp.float32) * scale
+    d_keys = jnp.einsum("hqk,hqd->hkd", d_scores, queries, preferred_element_type=jnp.float32) * scale
+    d_values = jnp.einsum("hqk,hqd->hkd", probs, d_mixed, preferred_element_type=jnp.float32)
+    d_joined = jnp.stack([d_queries, d_keys, d_values]).astype(jnp.bfloat16)
+    return d_joined.transpose(2, 1, 0, 3).reshape(total_len, -1)
+
+
+def by_sequence(
+    tokens,
+    cotangent,
+    seq_lengths,
+    combined_weight,
+    joined_bias,
+    attention_out_weight,
+    attention_out_bias,
+    expand_weight,
+    expand_bias,
+    contract_weight,
+    contract_bias,
+    norm_gains,
+    norm_shifts,
+):
+    n_layers, width, own_heads, _, head_dim = combined_weight.shape
+    n_tp, n_ctx = lax.axis_size("tp"), lax.axis_size("ctx")
+    n_rows = tokens.shape[1]
+    total_len = n_rows * n_ctx
+    own_seq = lax.axis_index("tp") * (tokens.shape[0] // n_tp) + lax.axis_index("ctx") // n_tp
+    key_valid = jnp.arange(total_len) < seq_lengths[own_seq]
+
+    flat_bias = jnp.concatenate(
+        [
+            joined_bias.transpose(0, 2, 1, 3).reshape(n_layers, 2, -1)[:, 0],
+            joined_bias.transpose(0, 2, 1, 3).reshape(n_layers, 2, -1)[:, 1],
+            expand_bias,
+        ],
+        axis=1,
+    )
+    flat_bias = lax.all_gather(flat_bias, "tp", axis=1)
+    own_cols = own_heads * head_dim
+    bias_q = flat_bias[..., :own_cols].reshape(n_layers, n_tp * own_heads, 1, head_dim)
+    bias_v = flat_bias[..., own_cols : 2 * own_cols].reshape(bias_q.shape)
+    bias_qkv = jnp.concatenate([bias_q, jnp.zeros_like(bias_q), bias_v], axis=2)
+    bias_qkv = bias_qkv.reshape(n_layers, -1).astype(jnp.float32)
+    bias_up = flat_bias[..., 2 * own_cols :].reshape(n_layers, -1).astype(jnp.float32)
+
+    fetched = []
+    last = None
+    for layer_idx in range(n_layers):
+        sources = (
+            (fetch_columns, combined_weight[layer_idx].reshape(width, -1)),
+            (fetch_rows, attention_out_weight[layer_idx]),
+            (fetch_columns, expand_weight[layer_idx]),
+            (fetch_rows, contract_weight[layer_idx]),
+        )
+        held = []
+        for fetch, weight in sources:
+            if last is not None:
+                weight = after(weight, last)
+            held.append(fetch(weight))
+            last = held[-1]
+        fetched.append(held)
+
+    hidden = rows_of(tokens, "tp", 0).reshape(-1, width).astype(jnp.float32)
+    saved = []
+    for layer_idx in range(n_layers):
+        w_qkv, w_out, w_up, w_down = fetched[layer_idx]
+        hidden_low = hidden.astype(jnp.bfloat16)
+        projected = (matmul(hidden_low, w_qkv) + bias_qkv[layer_idx]).astype(jnp.bfloat16)
+        mixed, attn_kept = attend(to_heads(projected, n_tp), key_valid, head_dim)
+        mixed = to_rows(mixed, n_tp)
+        branch = matmul(mixed, w_out)
+        normed, first_back = jax.vjp(
+            normalize,
+            hidden + branch + attention_out_bias[layer_idx],
+            norm_gains[layer_idx, 0].astype(jnp.float32),
+            norm_shifts[layer_idx, 0].astype(jnp.float32),
+        )
+        normed_low = normed.astype(jnp.bfloat16)
+        before = matmul(normed_low, w_up) + bias_up[layer_idx]
+        gated = smooth_gate(before).astype(jnp.bfloat16)
+        hidden, second_back = jax.vjp(
+            normalize,
+            normed + matmul(gated, w_down) + contract_bias[layer_idx],
+            norm_gains[layer_idx, 1].astype(jnp.float32),
+            norm_shifts[layer_idx, 1].astype(jnp.float32),
+        )
+        saved.append((hidden_low, attn_kept, mixed, normed_low, before, gated, first_back, second_back))
+
+    n_share = tokens.shape[0] // n_tp
+    outputs = lax.all_gather(
+        hidden.astype(jnp.bfloat16).reshape(n_share, n_rows, width), "tp", axis=0, tiled=True
+    ).astype(jnp.float32)
+
+    grad_now = rows_of(cotangent, "tp", 0).reshape(-1, width).astype(jnp.float32)
+    reduced = [None] * n_layers
+    small = [None] * n_layers
+    for layer_idx in reversed(range(n_layers)):
+        w_qkv, w_out, w_up, w_down = fetched[layer_idx]
+        hidden_low, attn_kept, mixed, normed_low, before, gated, first_back, second_back = saved[layer_idx]
+        d_resid_two, d_gain_two, d_shift_two = second_back(grad_now)
+        d_two_low = d_resid_two.astype(jnp.bfloat16)
+        d_down = matmul_tn(gated, d_two_low)
+        d_gated = matmul_nt(d_two_low, w_down)
+        d_before = jax.vjp(smooth_gate, before)[1](d_gated)[0].astype(jnp.bfloat16)
+        d_up = matmul_tn(normed_low, d_before)
+        d_normed = matmul_nt(d_before, w_up) + d_resid_two
+        d_resid_one, d_gain_one, d_shift_one = first_back(d_normed)
+        d_one_low = d_resid_one.astype(jnp.bfloat16)
+        d_out = matmul_tn(mixed, d_one_low)
+        d_mixed = matmul_nt(d_one_low, w_out).astype(jnp.bfloat16)
+        d_joined = attend_back(to_heads(d_mixed, n_tp), attn_kept, key_valid)
+        d_joined = to_rows(d_joined, n_tp)
+        d_qkv = matmul_tn(hidden_low, d_joined)
+        grad_now = matmul_nt(d_joined, w_qkv) + d_resid_one
+        early = [reduce_rows(d_down), reduce_columns(d_up), reduce_rows(d_out)]
+        late = reduce_columns(d_qkv)
+        reduced[layer_idx] = (late, early[2], early[1], early[0])
+        if layer_idx > 0:
+            chained = lax.optimization_barrier((grad_now,))
+            grad_now = chained[0]
+        small[layer_idx] = (
+            jnp.sum(d_joined.astype(jnp.float32), axis=0),
+            jnp.sum(d_resid_one, axis=0),
+            jnp.sum(d_before.astype(jnp.float32), axis=0),
+            jnp.sum(d_resid_two, axis=0),
+            d_gain_one,
+            d_gain_two,
+            d_shift_one,
+            d_shift_two,
+        )
+
+    tokens_grad = lax.all_gather(
+        grad_now.astype(jnp.bfloat16).reshape(n_share, n_rows, width), "tp", axis=0, tiled=True
+    ).astype(jnp.float32)
+    sizes = [entry.shape[0] for entry in small[0]]
+    packed = jnp.stack([jnp.concatenate(entry) for entry in small])
+    packed = lax.psum(packed, ("ctx", "tp"))
+    pieces = []
+    at = 0
+    for size in sizes:
+        pieces.append(packed[:, at : at + size])
+        at += size
+    d_bias = pieces[0].reshape(n_layers, n_tp * own_heads, 3, head_dim)[:, :, ::2, :]
+    whole = [[spread(entry) for entry in layer] for layer in reduced]
+    stacked = [jnp.stack([layer[member] for layer in whole]) for member in range(4)]
+    return (
+        outputs,
+        tokens_grad,
+        stacked[0].reshape(combined_weight.shape),
+        rows_of(d_bias, "tp", 1),
+        stacked[1],
+        pieces[1],
+        stacked[2],
+        rows_of(pieces[2], "tp", 1),
+        stacked[3],
+        pieces[3],
+        jnp.stack([pieces[4], pieces[5]], axis=1),
+        jnp.stack([pieces[6], pieces[7]], axis=1),
+    )
+
 
 def solution(mesh):
     placed = (
@@ -367,8 +622,14 @@
         P(),
         P(),
     )
+
+    def chosen(tokens, *rest):
+        n_seqs, n_ctx, n_tp = tokens.shape[0], mesh.shape["ctx"], mesh.shape["tp"]
+        whole_heads = n_seqs == n_ctx and n_seqs % n_tp == 0
+        return (by_sequence if whole_heads else on_device)(tokens, *rest)
+
     return jax.shard_map(
-        on_device,
+        chosen,
         mesh=mesh,
         in_specs=placed,
         out_specs=(

time: 1620 us -> 1480 us (0.914)
  waiting for transfers between devices: 1290 us -> 893 us
  blocking collectives: 42.2 us -> 261 us
  local copies, waits for them, and re-layouts: 28.2 us -> 92 us
  matrix products: 162 us -> 120 us
  starting transfers between devices: 2.82 us -> 19.9 us
    reduce_scatter x12 -> x14, waiting for transfers between devices: 641 us -> 334 us  [the longest x4 95.3 us: reduce_columns(): lax.psum_scatter(grad.astype(jnp.bfloat16), 'ctx', scatter_dimension=0, t...]
    all_gather x0 -> x13, blocking collectives: none -> 184 us  [the longest x4 66.8 us: fetch_columns(): part = lax.all_gather(rows_of(weight, 'ctx', 0), 'tp', axis=0)]
    all_gather x13 -> x14, waiting for transfers between devices: 492 us -> 329 us  [the longest x4 106 us: fetch_columns(): return lax.all_gather(part, 'ctx', axis=0, tiled=True)]
    all_to_all x0 -> x3, blocking collectives: none -> 77.1 us  [the longest x2 45.4 us: to_rows(): blocks = lax.all_to_all(blocks, 'ctx', 0, 0, tiled=True)]
    unnamed x26 -> x33, waiting for transfers between devices: 0.93 us -> 63.9 us
    all_to_all x0 -> x5, waiting for transfers between devices: none -> 44.6 us  [the longest x3 32.6 us: to_heads(): blocks = lax.all_to_all(blocks, 'ctx', 0, 0, tiled=True)]
    psum x2 -> x0, blocking collectives: 42.2 us -> none  [the longest x1 25.3 us: sum_layer(): lax.psum((grads[0], grads[1], grads[2], grads[3], grads[4], grads[5], gra...]
    dot_general x36, matrix products: 162 us -> 120 us  [the longest x8 30.9 us: matmul_tn(): lax.dot_general(left, right, (((0,), (0,)), ((), ())), preferred_element_...]
  transfers between devices with their start and end apart: 26 -> 36, of which waited for: 26 -> 32; matrix products, arithmetic and copies ran while one was open for 7% -> 15% of each run, Pallas kernels for 0% -> 0%
where the time goes in v1:
time: 1480 us; the launch traced here: 1470 us
  waiting for transfers between devices  893 us (60%)
  blocking collectives  261 us (18%)
  matrix products  120 us (8%)
  local copies, waits for them, and re-layouts  92 us (6%)
  other arithmetic  68.1 us (5%)
  starting transfers between devices  19.9 us (1%)
  between operations  16.8 us (1%)
    psum x1, waiting for transfers between devices, by_sequence(): packed = lax.psum(packed, ('ctx', 'tp'))  121 us
    all_gather x4, waiting for transfers between devices, fetch_columns(): return lax.all_gather(part, 'ctx', axis=0, tiled=True)  106 us
    reduce_scatter x4, waiting for transfers between devices, reduce_columns(): lax.psum_scatter(grad.astype(jnp.bfloat16), 'ctx', scatter_dimension=0, t...  95.3 us
    all_gather x4, waiting for transfers between devices, fetch_rows(): whole = lax.all_gather(part, 'ctx', axis=1, tiled=True)  85.5 us
    all_gather x4, waiting for transfers between devices, spread(): return lax.all_gather(part, 'ctx', axis=0, tiled=True).astype(jnp.float32)  84.1 us
    reduce_scatter x4, waiting for transfers between devices, reduce_rows(): return lax.psum_scatter(part, 'tp', scatter_dimension=0)  83.4 us
    reduce_scatter x2, waiting for transfers between devices, reduce_rows(): part = lax.psum_scatter(part, 'ctx', scatter_dimension=1, tiled=True)  80.8 us
    reduce_scatter x4, waiting for transfers between devices, reduce_columns(): return lax.psum_scatter(part, 'tp', scatter_dimension=0)  74.9 us
  transfers between devices with their start and end apart: 36, of which 32 were waited for; matrix products, arithmetic and copies ran while one was open for 15% of the time, Pallas kernels for 0%

profile of v1, /device:TPU:0, one launch (start us, length us, event | category | flops | bytes accessed | tf_op | source)
XLA Modules:
  0.0 1471.7 jit_solution(10536552753257911893)
XLA Ops:
  28.7 35.8 %all-gather.32.cloned.1.call-done = bf16[768,2304]{1,0:T(8,128)(2,1)} async-done(((bf16[96,2304]{1,0:T(8,128)(2,1)}), bf16[768,2304]{1,0:T(8,128)(2,1)}) %all-gather.32.cloned.1.call-update) | async-done | bytes 3538960 | tf_op jit(solution)/shard_map/all_gather | solution.py:365
  81.6 21.6 %all-gather.34.cloned.1.call-done = bf16[4,192,768]{2,1,0:T(8,128)(2,1)} async-done(((bf16[4,24,768]{2,1,0:T(8,128)(2,1)}), bf16[4,192,768]{2,1,0:T(8,128)(2,1)}) %all-gather.34.cloned.1.call-update) | async-done | bytes 1179664 | tf_op jit(solution)/shard_map/all_gather | solution.py:370
  125.9 35.5 %all-gather.36.cloned.1.call-done = bf16[768,3072]{1,0:T(8,128)(2,1)} async-done(((bf16[96,3072]{1,0:T(8,128)(2,1)}), bf16[768,3072]{1,0:T(8,128)(2,1)}) %all-gather.36.cloned.1.call-update) | async-done | bytes 4718608 | tf_op jit(solution)/shard_map/all_gather | solution.py:365
  179.5 39.4 %all-gather.38.cloned.1.call-done = bf16[4,768,768]{2,1,0:T(8,128)(2,1)} async-done(((bf16[4,96,768]{2,1,0:T(8,128)(2,1)}), bf16[4,768,768]{2,1,0:T(8,128)(2,1)}) %all-gather.38.cloned.1.call-update) | async-done | bytes 4718608 | tf_op jit(solution)/shard_map/all_gather | solution.py:370
  237.3 34.6 %all-gather.40.cloned.1.call-done = bf16[768,2304]{1,0:T(8,128)(2,1)} async-done(((bf16[96,2304]{1,0:T(8,128)(2,1)}), bf16[768,2304]{1,0:T(8,128)(2,1)}) %all-gather.40.cloned.1.call-update) | async-done | bytes 3538960 | tf_op jit(solution)/shard_map/all_gather | solution.py:365
  286.3 24.4 %all-gather.42.cloned.1.call-done = bf16[4,192,768]{2,1,0:T(8,128)(2,1)} async-done(((bf16[4,24,768]{2,1,0:T(8,128)(2,1)}), bf16[4,192,768]{2,1,0:T(8,128)(2,1)}) %all-gather.42.cloned.1.call-update) | async-done | bytes 1179664 | tf_op jit(solution)/shard_map/all_gather | solution.py:370
  356.0 23.8 %all-to-all-done = bf16[8,128,576]{1,2,0:T(8,128)(2,1)S(1)} async-done(((bf16[8,128,576]{1,2,0:T(8,128)(2,1)}), bf16[8,128,576]{1,2,0:T(8,128)(2,1)S(1)}, u32[]{:S(2)}, u32[]{:S(2)}) %all-to-all-start) | async-done | bytes 1179680 | tf_op jit(solution)/shard_map/all_to_all | solution.py:396
  446.4 31.8 %all_to_all.40 = bf16[8,128,576]{1,2,0:T(8,128)(2,1)S(1)} all-to-all(bf16[8,128,576]{1,2,0:T(8,128)(2,1)S(1)} %bitcast.328), channel_id=1, replica_groups=mesh['ctx'=8,'tp'=4] {'ctx'}, dimensions={0} | all-to-all | bytes 2359296 | tf_op jit(solution)/shard_map/all_to_all | solution.py:396
  575.3 26.2 %all_to_all.41 = bf16[8,128,576]{1,2,0:T(8,128)(2,1)S(1)} all-to-all(bf16[8,128,576]{1,2,0:T(8,128)(2,1)S(1)} %copy.205), channel_id=1, replica_groups=mesh['ctx'=8,'tp'=4] {'ctx'}, dimensions={0} | all-to-all | bytes 2359296 | tf_op jit(solution)/shard_map/all_to_all | solution.py:403
  712.5 23.3 %reduce-scatter.45.cloned.1.call-done = bf16[4,96,768]{2,1,0:T(8,128)(2,1)} async-done(((bf16[4,768,768]{2,1,0:T(8,128)(2,1)}), bf16[4,96,768]{2,1,0:T(8,128)(2,1)}) %reduce-scatter.45.cloned.1.call-update) | async-done | bytes 589840 | tf_op jit(solution)/shard_map/reduce_scatter | solution.py:384
  735.9 57.5 %reduce-scatter.41.cloned.1.call-done = bf16[4,96,768]{2,1,0:T(8,128)(2,1)} async-done(((bf16[4,768,768]{2,1,0:T(8,128)(2,1)}), bf16[4,96,768]{2,1,0:T(8,128)(2,1)}) %reduce-scatter.41.cloned.1.call-update) | async-done | bytes 589840 | tf_op jit(solution)/shard_map/reduce_scatter | solution.py:384
  793.5 40.5 %reduce-scatter.51.cloned.1.call-done = bf16[24,3072]{1,0:T(8,128)(2,1)} async-done(((bf16[192,3072]{1,0:T(8,128)(2,1)}), bf16[24,3072]{1,0:T(8,128)(2,1)}) %reduce-scatter.51.cloned.1.call-update) | async-done | bytes 147472
  851.4 22.8 %reduce-scatter.49.cloned.1.call-done = bf16[24,3072]{1,0:T(8,128)(2,1)} async-done(((bf16[192,3072]{1,0:T(8,128)(2,1)}), bf16[24,3072]{1,0:T(8,128)(2,1)}) %reduce-scatter.49.cloned.1.call-update) | async-done | bytes 147472
  880.0 46.3 %reduce-scatter.25.cloned.1.call-done = bf16[96,2304]{1,0:T(8,128)(2,1)} async-done(((bf16[768,2304]{1,0:T(8,128)(2,1)}), bf16[96,2304]{1,0:T(8,128)(2,1)}) %reduce-scatter.25.cloned.1.call-update) | async-done | bytes 442384 | tf_op jit(solution)/shard_map/reduce_scatter | solution.py:376
  928.8 49.0 %reduce-scatter.21.cloned.1.call-done = bf16[96,2304]{1,0:T(8,128)(2,1)} async-done(((bf16[768,2304]{1,0:T(8,128)(2,1)}), bf16[96,2304]{1,0:T(8,128)(2,1)}) %reduce-scatter.21.cloned.1.call-update) | async-done | bytes 442384 | tf_op jit(solution)/shard_map/reduce_scatter | solution.py:376
  980.3 22.1 %reduce-scatter.39.cloned.1.call-done = bf16[1,96,768]{2,1,0:T(8,128)(2,1)} async-done(((bf16[4,96,768]{2,1,0:T(8,128)(2,1)}), bf16[1,96,768]{2,1,0:T(8,128)(2,1)}) %reduce-scatter.39.cloned.1.call-update) | async-done | bytes 147472 | tf_op jit(solution)/shard_map/reduce_scatter | solution.py:378
  1002.5 23.0 %reduce-scatter.35.cloned.1.call-done = bf16[1,96,768]{2,1,0:T(8,128)(2,1)} async-done(((bf16[4,96,768]{2,1,0:T(8,128)(2,1)}), bf16[1,96,768]{2,1,0:T(8,128)(2,1)}) %reduce-scatter.35.cloned.1.call-update) | async-done | bytes 147472 | tf_op jit(solution)/shard_map/reduce_scatter | solution.py:378
  1025.5 22.6 %reduce-scatter.47.cloned.1.call-done = bf16[1,96,768]{2,1,0:T(8,128)(2,1)} async-done(((bf16[4,96,768]{2,1,0:T(8,128)(2,1)}), bf16[1,96,768]{2,1,0:T(8,128)(2,1)}) %reduce-scatter.47.cloned.1.call-update) | async-done | bytes 147472 | tf_op jit(solution)/shard_map/reduce_scatter | solution.py:385
  1048.1 22.4 %reduce-scatter.43.cloned.1.call-done = bf16[1,96,768]{2,1,0:T(8,128)(2,1)} async-done(((bf16[4,96,768]{2,1,0:T(8,128)(2,1)}), bf16[1,96,768]{2,1,0:T(8,128)(2,1)}) %reduce-scatter.43.cloned.1.call-update) | async-done | bytes 147472 | tf_op jit(solution)/shard_map/reduce_scatter | solution.py:385
  1101.1 26.9 %all-gather.48.cloned.1.call-done = bf16[8,128,768]{2,1,0:T(8,128)(2,1)} async-done(((bf16[2,128,768]{2,1,0:T(8,128)(2,1)}), bf16[8,128,768]{2,1,0:T(8,128)(2,1)}) %all-gather.48.cloned.1.call-update) | async-done | bytes 1572880 | tf_op jit(solution)/shard_map/all_gather | solution.py:537
  1131.4 121.4 %all-reduce.2.cloned.1.call-done = f32[2,9984]{1,0:T(2,128)} async-done(((f32[2,9984]{1,0:T(2,128)}), f32[2,9984]{1,0:T(2,128)}) %all-reduce.2.cloned.1.call-update) | async-done | bytes 79888 | tf_op jit(solution)/shard_map/psum | solution.py:584
  1286.8 26.8 %all-gather.50.cloned.1.call-done = bf16[8,128,768]{2,1,0:T(8,128)(2,1)} async-done(((bf16[2,128,768]{2,1,0:T(8,128)(2,1)}), bf16[8,128,768]{2,1,0:T(8,128)(2,1)}) %all-gather.50.cloned.1.call-update) | async-done | bytes 1572880 | tf_op jit(solution)/shard_map/all_gather | solution.py:579
  1382.8 26.0 %all-gather.52.cloned.1.call-done = bf16[1,768,768]{2,1,0:T(8,128)(2,1)} async-done(((bf16[1,96,768]{2,1,0:T(8,128)(2,1)}), bf16[1,768,768]{2,1,0:T(8,128)(2,1)}) %all-gather.52.cloned.1.call-update) | async-done | bytes 1179664 | tf_op jit(solution)/shard_map/all_gather | solution.py:389
  1434.7 26.0 %all-gather.56.cloned.1.call-done = bf16[1,768,768]{2,1,0:T(8,128)(2,1)} async-done(((bf16[1,96,768]{2,1,0:T(8,128)(2,1)}), bf16[1,768,768]{2,1,0:T(8,128)(2,1)}) %all-gather.56.cloned.1.call-update) | async-done | bytes 1179664 | tf_op jit(solution)/shard_map/all_gather | solution.py:389
  (545 shorter events, 625.3 us)
Async XLA Ops:
  286.2 124.7 %all-gather.44.cloned.1.call-start = ((), (), s32[]{:S(2)}) async-start(), calls=%async_computation.30 | async-start | bytes 5308416 | tf_op jit(solution)/shard_map/all_gather | solution.py:365
  542.5 165.9 %reduce-scatter.37.cloned.1.call-start = ((), (), s32[]{:S(2)}) async-start(), calls=%async_computation.43 | async-start | bytes 5308416 | tf_op jit(solution)/shard_map/reduce_scatter | solution.py:376
  548.0 162.4 %reduce-scatter.33.cloned.1.call-start = ((), (), s32[]{:S(2)}) async-start(), calls=%async_computation.41 | async-start | bytes 5308416 | tf_op jit(solution)/shard_map/reduce_scatter | solution.py:376
  617.8 118.0 %reduce-scatter.45.cloned.1.call-start = ((), (), s32[]{:S(2)}) async-start(), calls=%async_computation.47 | async-start | bytes 5308416 | tf_op jit(solution)/shard_map/reduce_scatter | solution.py:384
  625.0 168.4 %reduce-scatter.41.cloned.1.call-start = ((), (), s32[]{:S(2)}) async-start(), calls=%async_computation.45 | async-start | bytes 5308416 | tf_op jit(solution)/shard_map/reduce_scatter | solution.py:384
  631.8 202.2 %reduce-scatter.51.cloned.1.call-start = ((), (), s32[]{:S(2)}) async-start(), calls=%async_computation.54 | async-start | bytes 1327104
  635.6 238.7 %reduce-scatter.49.cloned.1.call-start = ((), (), s32[]{:S(2)}) async-start(), calls=%async_computation.53 | async-start | bytes 1327104
  651.8 274.5 %reduce-scatter.25.cloned.1.call-start = ((), (), s32[]{:S(2)}) async-start(), calls=%async_computation.36 | async-start | bytes 3981312 | tf_op jit(solution)/shard_map/reduce_scatter | solution.py:376
  656.2 321.5 %reduce-scatter.21.cloned.1.call-start = ((), (), s32[]{:S(2)}) async-start(), calls=%async_computation.34 | async-start | bytes 3981312 | tf_op jit(solution)/shard_map/reduce_scatter | solution.py:376
  708.3 294.1 %reduce-scatter.39.cloned.1.call-start = ((), (), s32[]{:S(2)}) async-start(), calls=%async_computation.44 | async-start | bytes 737280 | tf_op jit(solution)/shard_map/reduce_scatter | solution.py:378
  710.4 315.1 %reduce-scatter.35.cloned.1.call-start = ((), (), s32[]{:S(2)}) async-start(), calls=%async_computation.42 | async-start | bytes 737280 | tf_op jit(solution)/shard_map/reduce_scatter | solution.py:378
  712.5 335.6 %reduce-scatter.47.cloned.1.call-start = ((), (), s32[]{:S(2)}) async-start(), calls=%async_computation.48 | async-start | bytes 737280 | tf_op jit(solution)/shard_map/reduce_scatter | solution.py:385
  735.8 334.7 %reduce-scatter.43.cloned.1.call-start = ((), (), s32[]{:S(2)}) async-start(), calls=%async_computation.46 | async-start | bytes 737280 | tf_op jit(solution)/shard_map/reduce_scatter | solution.py:385
  793.4 297.6 %reduce-scatter.31.cloned.1.call-start = ((), (), s32[]{:S(2)}) async-start(), calls=%async_computation.40 | async-start | bytes 184320 | tf_op jit(solution)/shard_map/reduce_scatter | solution.py:385
  835.7 292.3 %all-gather.48.cloned.1.call-start = ((), (), s32[]{:S(2)}) async-start(), calls=%async_computation.32 | async-start | bytes 1966080 | tf_op jit(solution)/shard_map/all_gather | solution.py:537
  838.5 414.3 %all-reduce.2.cloned.1.call-start = ((), (), s32[]{:S(2)}) async-start(), calls=%async_computation.38 | async-start | bytes 159744 | tf_op jit(solution)/shard_map/psum | solution.py:584
  851.4 424.8 %reduce-scatter.29.cloned.1.call-start = ((), (), s32[]{:S(2)}) async-start(), calls=%async_computation.39 | async-start | bytes 184320 | tf_op jit(solution)/shard_map/reduce_scatter | solution.py:385
  875.9 437.7 %all-gather.50.cloned.1.call-start = ((), (), s32[]{:S(2)}) async-start(), calls=%async_computation.33 | async-start | bytes 1966080 | tf_op jit(solution)/shard_map/all_gather | solution.py:579
  879.9 456.7 %reduce-scatter.27.cloned.1.call-start = ((), (), s32[]{:S(2)}) async-start(), calls=%async_computation.37 | async-start | bytes 614400 | tf_op jit(solution)/shard_map/reduce_scatter | solution.py:378
  928.7 429.8 %reduce-scatter.23.cloned.1.call-start = ((), (), s32[]{:S(2)}) async-start(), calls=%async_computation.35 | async-start | bytes 614400 | tf_op jit(solution)/shard_map/reduce_scatter | solution.py:378
  980.2 402.6 %all-gather.54.cloned.1.call-start = ((), (), s32[]{:S(2)}) async-start(), calls=%async_computation.50 | async-start | bytes 1327104 | tf_op jit(solution)/shard_map/all_gather | solution.py:389
  1002.4 406.4 %all-gather.52.cloned.1.call-start = ((), (), s32[]{:S(2)}) async-start(), calls=%async_computation.49 | async-start | bytes 1327104 | tf_op jit(solution)/shard_map/all_gather | solution.py:389
  1025.5 409.2 %all-gather.58.cloned.1.call-start = ((), (), s32[]{:S(2)}) async-start(), calls=%async_computation.52 | async-start | bytes 1327104 | tf_op jit(solution)/shard_map/all_gather | solution.py:389
  1048.1 412.5 %all-gather.56.cloned.1.call-start = ((), (), s32[]{:S(2)}) async-start(), calls=%async_computation.51 | async-start | bytes 1327104 | tf_op jit(solution)/shard_map/all_gather | solution.py:389
  (125 other events, 3133.1 us)
Sparse Core Ops, SparseCore 0:
  28.7 35.7 all-gather.31
  78.9 24.3 all-gather.33
  122.8 38.5 all-gather.35
  179.6 39.3 all-gather.37
  237.4 34.4 all-gather.39
  286.4 24.3 all-gather.41
  329.3 48.0 all-gather.43
  428.7 50.7 all-gather.45
  548.1 67.9 reduce-scatter.36
  620.4 57.9 reduce-scatter.32
  681.9 53.8 reduce-scatter.44
  739.5 53.8 reduce-scatter.40
  797.2 36.7 reduce-scatter.50
  837.4 36.7 reduce-scatter.48
  878.2 48.0 reduce-scatter.24
  929.6 48.0 reduce-scatter.20
  980.4 21.8 reduce-scatter.38
  1092.7 35.2 all-gather.47
  1134.5 118.1 all-reduce.1
  1278.3 35.2 all-gather.49
  1360.4 22.3 all-gather.53
  1384.7 24.0 all-gather.51
  1410.6 24.0 all-gather.57
  1436.5 24.0 all-gather.55
  (7 shorter events, 139.2 us)

commit v2 on v1

--- a/solution.py
+++ b/solution.py
@@ -359,34 +359,43 @@
     return lax.optimization_barrier((value,) + earlier)[0]
 
 
-def fetch_columns(weight):
-    part = lax.all_gather(rows_of(weight, "ctx", 0), "tp", axis=0)
-    part = part.transpose(1, 0, 2).reshape(part.shape[1], -1)
-    return lax.all_gather(part, "ctx", axis=0, tiled=True)
-
-
-def fetch_rows(weight):
-    part = lax.all_gather(rows_of(weight, "ctx", 0), "tp", axis=0)
+def padded(array, width):
+    return jnp.pad(array, [(0, 0)] * (array.ndim - 1) + [(0, width - array.shape[-1])])
+
+
+def side_by_side(part):
+    return part.transpose(1, 0, 2).reshape(part.shape[1], -1)
+
+
+def fetch_columns(part):
+    return lax.all_gather(side_by_side(part), "ctx", axis=0, tiled=True)
+
+
+def fetch_rows(part):
     whole = lax.all_gather(part, "ctx", axis=1, tiled=True)
     return whole.reshape(-1, whole.shape[2])
 
 
-def reduce_columns(grad):
-    n_tp = lax.axis_size("tp")
-    part = lax.psum_scatter(grad.astype(jnp.bfloat16), "ctx", scatter_dimension=0, tiled=True)
-    part = part.reshape(part.shape[0], n_tp, -1).transpose(1, 0, 2)
-    return lax.psum_scatter(part, "tp", scatter_dimension=0)
-
-
-def reduce_rows(grad):
-    n_tp = lax.axis_size("tp")
-    part = grad.astype(jnp.bfloat16).reshape(n_tp, -1, grad.shape[1])
-    part = lax.psum_scatter(part, "ctx", scatter_dimension=1, tiled=True)
-    return lax.psum_scatter(part, "tp", scatter_dimension=0)
-
-
-def spread(part):
-    return lax.all_gather(part, "ctx", axis=0, tiled=True).astype(jnp.float32)
+def blocks_of_columns(grad, n_ctx, n_tp):
+    blocks = grad.astype(jnp.bfloat16).reshape(n_ctx, grad.shape[0] // n_ctx, n_tp, -1)
+    return blocks.transpose(0, 2, 1, 3)
+
+
+def blocks_of_rows(grad, n_ctx, n_tp):
+    blocks = grad.astype(jnp.bfloat16).reshape(n_tp, n_ctx, -1, grad.shape[1])
+    return blocks.transpose(1, 0, 2, 3)
+
+
+def sum_blocks(blocks, axis_name):
+    blocks = blocks.reshape(blocks.shape[0], -1, blocks.shape[-1])
+    moved = lax.all_to_all(blocks, axis_name, 0, 0, tiled=True)
+    return jnp.sum(moved.astype(jnp.float32), axis=0)
+
+
+def sum_everywhere(small):
+    for axis_name in ("tp", "ctx"):
+        small = jnp.sum(lax.all_gather(small, axis_name, axis=0), axis=0)
+    return small
 
 
 def to_heads(rows, n_groups):
@@ -490,31 +499,43 @@
     bias_qkv = bias_qkv.reshape(n_layers, -1).astype(jnp.float32)
     bias_up = flat_bias[..., 2 * own_cols :].reshape(n_layers, -1).astype(jnp.float32)
 
+    ends = [0]
+
+    def fetch_parts(layer_idx, *earlier):
+        sources = (
+            padded(rows_of(combined_weight[layer_idx].reshape(width, -1), "ctx", 0), width),
+            rows_of(attention_out_weight[layer_idx], "ctx", 0),
+            rows_of(expand_weight[layer_idx], "ctx", 0),
+            rows_of(contract_weight[layer_idx], "ctx", 0),
+        )
+        del ends[1:]
+        for source in sources:
+            ends.append(ends[-1] + source.shape[0])
+        part = lax.all_gather(after(jnp.concatenate(sources, axis=0), *earlier), "tp", axis=0)
+        own = [part[:, ends[i] : ends[i + 1]] for i in range(4)]
+        own[0] = own[0][:, :, : 3 * own_cols]
+        return own
+
     fetched = []
-    last = None
-    for layer_idx in range(n_layers):
-        sources = (
-            (fetch_columns, combined_weight[layer_idx].reshape(width, -1)),
-            (fetch_rows, attention_out_weight[layer_idx]),
-            (fetch_columns, expand_weight[layer_idx]),
-            (fetch_rows, contract_weight[layer_idx]),
-        )
-        held = []
-        for fetch, weight in sources:
-            if last is not None:
-                weight = after(weight, last)
-            held.append(fetch(weight))
-            last = held[-1]
-        fetched.append(held)
+    own = fetch_parts(0)
+    w_qkv = fetch_columns(own[0])
 
     hidden = rows_of(tokens, "tp", 0).reshape(-1, width).astype(jnp.float32)
     saved = []
     for layer_idx in range(n_layers):
-        w_qkv, w_out, w_up, w_down = fetched[layer_idx]
         hidden_low = hidden.astype(jnp.bfloat16)
         projected = (matmul(hidden_low, w_qkv) + bias_qkv[layer_idx]).astype(jnp.bfloat16)
+        later = [after(part, projected) for part in own[1:]]
+        w_out, w_up = fetch_rows(later[0]), fetch_columns(later[1])
+        w_down = fetch_rows(later[2])
+        fetched.append((w_qkv, w_out, w_up, w_down))
+        if layer_idx + 1 < n_layers:
+            own = fetch_parts(layer_idx + 1, projected)
         mixed, attn_kept = attend(to_heads(projected, n_tp), key_valid, head_dim)
         mixed = to_rows(mixed, n_tp)
+        if layer_idx + 1 < n_layers:
+            own = [after(part, mixed) for part in own]
+            w_qkv = fetch_columns(own[0])
         branch = matmul(mixed, w_out)
         normed, first_back = jax.vjp(
             normalize,
@@ -541,6 +562,7 @@
     grad_now = rows_of(cotangent, "tp", 0).reshape(-1, width).astype(jnp.float32)
     reduced = [None] * n_layers
     small = [None] * n_layers
+    summed_before = None
     for layer_idx in reversed(range(n_layers)):
         w_qkv, w_out, w_up, w_down = fetched[layer_idx]
         hidden_low, attn_kept, mixed, normed_low, before, gated, first_back, second_back = saved[layer_idx]
@@ -556,15 +578,22 @@
         d_out = matmul_tn(mixed, d_one_low)
         d_mixed = matmul_nt(d_one_low, w_out).astype(jnp.bfloat16)
         d_joined = attend_back(to_heads(d_mixed, n_tp), attn_kept, key_valid)
+        if summed_before is not None:
+            d_joined, summed_before = lax.optimization_barrier((d_joined, summed_before))
         d_joined = to_rows(d_joined, n_tp)
         d_qkv = matmul_tn(hidden_low, d_joined)
         grad_now = matmul_nt(d_joined, w_qkv) + d_resid_one
-        early = [reduce_rows(d_down), reduce_columns(d_up), reduce_rows(d_out)]
-        late = reduce_columns(d_qkv)
-        reduced[layer_idx] = (late, early[2], early[1], early[0])
-        if layer_idx > 0:
-            chained = lax.optimization_barrier((grad_now,))
-            grad_now = chained[0]
+        blocks = [
+            padded(blocks_of_columns(d_qkv, n_ctx, n_tp), width),
+            blocks_of_rows(d_out, n_ctx, n_tp),
+            blocks_of_columns(d_up, n_ctx, n_tp),
+            blocks_of_rows(d_down, n_ctx, n_tp),
+        ]
+        summed = sum_blocks(jnp.concatenate(blocks, axis=2), "ctx")
+        summed = summed.astype(jnp.bfloat16)
+        summed_before = summed
+        summed = sum_blocks(summed.reshape(n_tp, -1, width), "tp").astype(jnp.bfloat16)
+        reduced[layer_idx] = lax.all_gather(summed, "ctx", axis=0)
         small[layer_idx] = (
             jnp.sum(d_joined.astype(jnp.float32), axis=0),
             jnp.sum(d_resid_one, axis=0),
@@ -581,14 +610,18 @@
     ).astype(jnp.float32)
     sizes = [entry.shape[0] for entry in small[0]]
     packed = jnp.stack([jnp.concatenate(entry) for entry in small])
-    packed = lax.psum(packed, ("ctx", "tp"))
+    packed = sum_everywhere(packed)
     pieces = []
     at = 0
     for size in sizes:
         pieces.append(packed[:, at : at + size])
         at += size
     d_bias = pieces[0].reshape(n_layers, n_tp * own_heads, 3, head_dim)[:, :, ::2, :]
-    whole = [[spread(entry) for entry in layer] for layer in reduced]
+    whole = []
+    for layer in reduced:
+        pieces_of = [layer[:, ends[i] : ends[i + 1]].astype(jnp.float32) for i in range(4)]
+        pieces_of[0] = pieces_of[0][:, :, : 3 * own_cols]
+        whole.append([piece.reshape(-1, piece.shape[2]) for piece in pieces_of])
     stacked = [jnp.stack([layer[member] for layer in whole]) for member in range(4)]
     return (
         outputs,

time: 1480 us -> 1180 us (0.80)
  waiting for transfers between devices: 893 us -> 577 us
  blocking collectives: 261 us -> 132 us
  local copies, waits for them, and re-layouts: 92 us -> 175 us
  other arithmetic: 68.1 us -> 105 us
  starting transfers between devices: 19.9 us -> 36.5 us
    reduce_scatter x14 -> x0, waiting for transfers between devices: 334 us -> none  [the longest x4 95.3 us: reduce_columns(): lax.psum_scatter(grad.astype(jnp.bfloat16), 'ctx', scatter_dimension=0, t...]
    all_to_all x0 -> x3, waiting for transfers between devices: none -> 324 us  [sum_blocks(): moved = lax.all_to_all(blocks, axis_name, 0, 0, tiled=True)]
    all_gather x12 -> x2, blocking collectives: 171 us -> 27.5 us  [sum_everywhere(): small = jnp.sum(lax.all_gather(small, axis_name, axis=0), axis=0)]
    psum x1 -> x0, waiting for transfers between devices: 121 us -> none  [by_sequence(): packed = lax.psum(packed, ('ctx', 'tp'))]
    unnamed x33 -> x14, waiting for transfers between devices: 63.9 us -> 1.92 us
    reshape x8 -> x17, local copies, waits for them, and re-layouts: 11.2 us -> 70 us  [the longest x8 55 us: blocks_of_columns(): grad.astype(jnp.bfloat16).reshape(n_ctx, grad.shape[0] // n_ctx, n_tp, -1)]
    all_gather x8, waiting for transfers between devices: 190 us -> 135 us  [the longest x4 89 us: fetch_columns(): return lax.all_gather(side_by_side(part), 'ctx', axis=0, tiled=True)]
    all_to_all x0 -> x1, blocking collectives: none -> 46.7 us  [sum_blocks(): moved = lax.all_to_all(blocks, axis_name, 0, 0, tiled=True)]
  transfers between devices with their start and end apart: 36 -> 22, of which waited for: 32 -> 13; matrix products, arithmetic and copies ran while one was open for 15% -> 23% of each run, Pallas kernels for 0% -> 0%
where the time goes in v2:
time: 1180 us; the launch traced here: 1170 us
  waiting for transfers between devices  577 us (49%)
  local copies, waits for them, and re-layouts  175 us (15%)
  blocking collectives  132 us (11%)
  matrix products  126 us (11%)
  other arithmetic  105 us (9%)
  starting transfers between devices  36.5 us (3%)
  between operations  16.2 us (1%)
    all_to_all x3, waiting for transfers between devices, sum_blocks(): moved = lax.all_to_all(blocks, axis_name, 0, 0, tiled=True)  324 us
    all_gather x4, waiting for transfers between devices, fetch_columns(): return lax.all_gather(side_by_side(part), 'ctx', axis=0, tiled=True)  89 us
    all_gather x4, waiting for transfers between devices, fetch_rows(): whole = lax.all_gather(part, 'ctx', axis=1, tiled=True)  79.2 us
    reshape x8, local copies, waits for them, and re-layouts, blocks_of_columns(): grad.astype(jnp.bfloat16).reshape(n_ctx, grad.shape[0] // n_ctx, n_tp, -1)  55 us
    all_to_all x1, blocking collectives, sum_blocks(): moved = lax.all_to_all(blocks, axis_name, 0, 0, tiled=True)  46.7 us
    all_gather x2, waiting for transfers between devices, fetch_parts(): lax.all_gather(after(jnp.concatenate(sources, axis=0), *earlier), 'tp', a...  45.6 us
    dot_general x8, matrix products, matmul(): return jnp.dot(left, right, preferred_element_type=jnp.float32)  34.5 us
    all_to_all x2, blocking collectives, to_heads(): blocks = lax.all_to_all(blocks, 'ctx', 0, 0, tiled=True)  34.2 us
  transfers between devices with their start and end apart: 22, of which 13 were waited for; matrix products, arithmetic and copies ran while one was open for 23% of the time, Pallas kernels for 0%

profile of v2, /device:TPU:0, one launch (start us, length us, event | category | flops | bytes accessed | tf_op | source)
XLA Modules:
  0.0 1167.5 jit_solution(11960361908480413858)
XLA Ops:
  24.0 45.6 %all-gather.44.cloned.1.call-done = bf16[1248,768]{1,0:T(8,128)(2,1)} async-done(((bf16[312,768]{1,0:T(8,128)(2,1)}), bf16[1248,768]{1,0:T(8,128)(2,1)}) %all-gather.44.cloned.1.call-update) | async-done | bytes 1916944 | tf_op jit(solution)/shard_map/all_gather | solution.py:514
  73.8 13.1 %all-gather.1 = bf16[2,4608]{1,0:T(2,128)(2,1)S(1)} all-gather(bf16[2,1152]{1,0:T(2,128)(2,1)S(1)} %concatenate.27), channel_id=3, replica_groups=mesh['ctx'=8,'tp'=4] {'tp'}, dimensions={1}, use_global_device_ids=true | all-gather | bytes 23040 | tf_op jit(solution)/shard_map/all_gather | solution.py:494
  89.8 15.3 %all-gather.24.cloned.1.call-done = bf16[768,2304]{1,0:T(8,128)(2,1)} async-done(((bf16[96,2304]{1,0:T(8,128)(2,1)}), bf16[768,2304]{1,0:T(8,128)(2,1)}) %all-gather.24.cloned.1.call-update) | async-done | bytes 3538960 | tf_op jit(solution)/shard_map/all_gather | solution.py:371
  123.3 15.1 %all-to-all-done = bf16[8,128,576]{1,2,0:T(8,128)(2,1)S(1)} async-done(((bf16[8,128,576]{1,2,0:T(8,128)(2,1)}), bf16[8,128,576]{1,2,0:T(8,128)(2,1)S(1)}, u32[]{:S(2)}, u32[]{:S(2)}) %all-to-all-start) | async-done | bytes 1179680 | tf_op jit(solution)/shard_map/all_to_all | solution.py:405
  154.6 10.9 all_to_all.60
  182.4 37.5 %all-gather.28.cloned.1.call-done = bf16[768,3072]{1,0:T(8,128)(2,1)} async-done(((bf16[96,3072]{1,0:T(8,128)(2,1)}), bf16[768,3072]{1,0:T(8,128)(2,1)}) %all-gather.28.cloned.1.call-update) | async-done | bytes 4718608 | tf_op jit(solution)/shard_map/all_gather | solution.py:371
  225.4 35.8 %all-gather.30.cloned.1.call-done = bf16[4,768,768]{2,1,0:T(8,128)(2,1)} async-done(((bf16[4,96,768]{2,1,0:T(8,128)(2,1)}), bf16[4,768,768]{2,1,0:T(8,128)(2,1)}) %all-gather.30.cloned.1.call-update) | async-done | bytes 4718608 | tf_op jit(solution)/shard_map/all_gather | solution.py:375
  266.8 30.8 %all-gather.32.cloned.1.call-done = bf16[768,2304]{1,0:T(8,128)(2,1)} async-done(((bf16[96,2304]{1,0:T(8,128)(2,1)}), bf16[768,2304]{1,0:T(8,128)(2,1)}) %all-gather.32.cloned.1.call-update) | async-done | bytes 3538960 | tf_op jit(solution)/shard_map/all_gather | solution.py:371
  313.1 23.1 %all_to_all.61 = bf16[8,128,576]{1,2,0:T(8,128)(2,1)S(1)} all-to-all(bf16[8,128,576]{1,2,0:T(8,128)(2,1)S(1)} %bitcast.349), channel_id=1, replica_groups=mesh['ctx'=8,'tp'=4] {'ctx'}, dimensions={0} | all-to-all | bytes 2359296 | tf_op jit(solution)/shard_map/all_to_all | solution.py:405
  357.3 11.8 %all-to-all-done.3 = bf16[8,128,192]{1,2,0:T(8,128)(2,1)S(1)} async-done(((bf16[8,128,192]{1,2,0:T(8,128)(2,1)}), bf16[8,128,192]{1,2,0:T(8,128)(2,1)S(1)}, u32[]{:S(2)}, u32[]{:S(2)}) %all-to-all-start.3) | async-done | bytes 393248 | tf_op jit(solution)/shard_map/all_to_all | solution.py:412
  383.8 35.7 %all-gather.38.cloned.1.call-done = bf16[4,768,768]{2,1,0:T(8,128)(2,1)} async-done(((bf16[4,96,768]{2,1,0:T(8,128)(2,1)}), bf16[4,768,768]{2,1,0:T(8,128)(2,1)}) %all-gather.38.cloned.1.call-update) | async-done | bytes 4718608 | tf_op jit(solution)/shard_map/all_gather | solution.py:375
  441.7 11.1 all_to_all.62
  496.1 10.2 reshape.420
  537.9 9.1 reshape.418
  586.0 148.0 %all-to-all-done.7 = bf16[8,1248,768]{2,1,0:T(8,128)(2,1)} async-done(((bf16[8,1248,768]{2,1,0:T(8,128)(2,1)}), bf16[8,1248,768]{2,1,0:T(8,128)(2,1)}, u32[]{:S(2)}, u32[]{:S(2)}) %all-to-all-start.7) | async-done | bytes 15335456 | tf_op jit(solution)/shard_map/all_to_all | solution.py:391
  734.0 10.1 reduce_sum.478
  755.5 10.3 all-to-all-done.8
  780.6 9.7 reshape.429
  802.7 9.1 reshape.427
  838.2 176.0 %all-to-all-done.9 = bf16[8,1248,768]{2,1,0:T(8,128)(2,1)} async-done(((bf16[8,1248,768]{2,1,0:T(8,128)(2,1)}), bf16[8,1248,768]{2,1,0:T(8,128)(2,1)}, u32[]{:S(2)}, u32[]{:S(2)}) %all-to-all-start.9) | async-done | bytes 15335456 | tf_op jit(solution)/shard_map/all_to_all | solution.py:391
  1014.1 10.1 reduce_sum.479
  1024.2 46.7 %all_to_all.63 = bf16[4,312,768]{2,1,0:T(8,128)(2,1)} all-to-all(bf16[4,312,768]{2,1,0:T(8,128)(2,1)} %bitcast.333), channel_id=1, replica_groups=mesh['ctx'=8,'tp'=4] {'tp'}, dimensions={0} | all-to-all | bytes 3833856 | tf_op jit(solution)/shard_map/all_to_all | solution.py:391
  1097.3 14.4 %all-gather.7 = f32[4,2,9984]{2,1,0:T(2,128)S(1)} all-gather(f32[1,2,9984]{2,1,0:T(2,128)S(1)} %maximum_bitcast_fusion.2), channel_id=7, replica_groups=mesh['ctx'=8,'tp'=4] {'tp'}, dimensions={0}, use_global_device_ids=true | all-gather | bytes 399360 | tf_op jit(solution)/shard_map/all_gather | solution.py:397
  1111.8 13.1 %all-gather.8 = f32[8,2,9984]{2,1,0:T(2,128)S(1)} all-gather(f32[1,2,9984]{2,1,0:T(2,128)S(1)} %bitcast.403), channel_id=8, replica_groups=mesh['ctx'=8,'tp'=4] {'ctx'}, dimensions={0}, use_global_device_ids=true | all-gather | bytes 718848 | tf_op jit(solution)/shard_map/all_gather | solution.py:397
  (548 shorter events, 398.7 us)
Async XLA Ops:
  7.2 62.3 %all-gather.44.cloned.1.call-start = ((), (), s32[]{:S(2)}) async-start(), calls=%async_computation.22 | async-start | bytes 2396160 | tf_op jit(solution)/shard_map/all_gather | solution.py:514
  23.9 81.1 %all-gather.24.cloned.1.call-start = ((), (), s32[]{:S(2)}) async-start(), calls=%async_computation.12 | async-start | bytes 3981312 | tf_op jit(solution)/shard_map/all_gather | solution.py:371
  72.1 93.9 %all-gather.46.cloned.1.call-start = ((), (), s32[]{:S(2)}) async-start(), calls=%async_computation.23 | async-start | bytes 2396160 | tf_op jit(solution)/shard_map/all_gather | solution.py:514
  110.5 68.2 %all-gather.26.cloned.1.call-start = ((), (), s32[]{:S(2)}) async-start(), calls=%async_computation.13 | async-start | bytes 1327104 | tf_op jit(solution)/shard_map/all_gather | solution.py:375
  111.2 108.7 %all-gather.28.cloned.1.call-start = ((), (), s32[]{:S(2)}) async-start(), calls=%async_computation.14 | async-start | bytes 5308416 | tf_op jit(solution)/shard_map/all_gather | solution.py:371
  113.1 148.1 %all-gather.30.cloned.1.call-start = ((), (), s32[]{:S(2)}) async-start(), calls=%async_computation.15 | async-start | bytes 5308416 | tf_op jit(solution)/shard_map/all_gather | solution.py:375
  118.1 20.3 %all-to-all-start = ((bf16[8,128,576]{1,2,0:T(8,128)(2,1)}), bf16[8,128,576]{1,2,0:T(8,128)(2,1)S(1)}, u32[]{:S(2)}, u32[]{:S(2)}) async-start(bf16[8,128,576]{1,2,0:T(8,128)(2,1)} %bitcast.10), calls=%async_computation | async-start | bytes 2359296 | tf_op jit(solution)/shard_map/all_to_all | solution.py:405
  121.7 176.0 %all-gather.32.cloned.1.call-start = ((), (), s32[]{:S(2)}) async-start(), calls=%async_computation.16 | async-start | bytes 3981312 | tf_op jit(solution)/shard_map/all_gather | solution.py:371
  123.3 221.9 %copy-start.49 = (pred[1024]{0:T(1024)(128)(4,1)}, pred[1024]{0:T(1024)(128)(4,1)S(1)}, u32[]{:S(2)}) copy-start(pred[1024]{0:T(1024)(128)(4,1)S(1)} %iota_compare_fusion.2) | copy-start | bytes 3076
  168.6 201.6 %all-gather.34.cloned.1.call-start = ((), (), s32[]{:S(2)}) async-start(), calls=%async_computation.17 | async-start | bytes 1327104 | tf_op jit(solution)/shard_map/all_gather | solution.py:375
  171.0 126.6 %copy-start.81 = (f32[768]{0:T(1024)}, f32[768]{0:T(1024)S(1)}, u32[]{:S(2)}) copy-start(f32[768]{0:T(1024)S(1)} %get-tuple-element.124) | copy-start | bytes 9220
  301.9 76.4 %all-gather.36.cloned.1.call-start = ((), (), s32[]{:S(2)}) async-start(), calls=%async_computation.18 | async-start | bytes 5308416 | tf_op jit(solution)/shard_map/all_gather | solution.py:371
  305.0 114.5 %all-gather.38.cloned.1.call-start = ((), (), s32[]{:S(2)}) async-start(), calls=%async_computation.19 | async-start | bytes 5308416 | tf_op jit(solution)/shard_map/all_gather | solution.py:375
  353.0 16.0 %all-to-all-start.3 = ((bf16[8,128,192]{1,2,0:T(8,128)(2,1)}), bf16[8,128,192]{1,2,0:T(8,128)(2,1)S(1)}, u32[]{:S(2)}, u32[]{:S(2)}) async-start(bf16[8,128,192]{1,2,0:T(8,128)(2,1)} %copy.285), calls=%async_computation.3 | async-start | bytes 786432 | tf_op jit(solution)/shard_map/all_to_all | solution.py:412
  481.7 31.8 %all-to-all-start.5 = ((bf16[8,128,576]{1,2,0:T(8,128)(2,1)}), bf16[8,128,576]{1,2,0:T(8,128)(2,1)S(1)}, u32[]{:S(2)}, u32[]{:S(2)}) async-start(bf16[8,128,576]{1,2,0:T(8,128)(2,1)} %copy.295), calls=%async_computation.5 | async-start | bytes 2359296 | tf_op jit(solution)/shard_map/all_to_all | solution.py:412
  533.6 26.2 %all-to-all-start.6 = ((bf16[8,128,192]{1,2,0:T(8,128)(2,1)}), bf16[8,128,192]{1,2,0:T(8,128)(2,1)S(1)}, u32[]{:S(2)}, u32[]{:S(2)}) async-start(bf16[8,128,192]{1,2,0:T(8,128)(2,1)} %bitcast.51), calls=%async_computation.6 | async-start | bytes 786432 | tf_op jit(solution)/shard_map/all_to_all | solution.py:405
  559.7 174.3 %all-to-all-start.7 = ((bf16[8,1248,768]{2,1,0:T(8,128)(2,1)}), bf16[8,1248,768]{2,1,0:T(8,128)(2,1)}, u32[]{:S(2)}, u32[]{:S(2)}) async-start(bf16[8,1248,768]{2,1,0:T(8,128)(2,1)} %bitcast.305), calls=%async_computation.7 | async-start | bytes 30670848 | tf_op jit(solution)/shard_map/all_to_all | solution.py:391
  745.3 20.5 %all-to-all-start.8 = ((bf16[8,128,576]{1,2,0:T(8,128)(2,1)}), bf16[8,128,576]{1,2,0:T(8,128)(2,1)S(1)}, u32[]{:S(2)}, u32[]{:S(2)}) async-start(bf16[8,128,576]{1,2,0:T(8,128)(2,1)} %copy_bitcast_fusion.6), calls=%async_computation.8 | async-start | bytes 2359296 | tf_op jit(solution)/shard_map/all_to_all | solution.py:412
  765.9 58.6 %all-to-all-start.11 = ((bf16[4,312,768]{2,1,0:T(8,128)(2,1)}), bf16[4,312,768]{2,1,0:T(8,128)(2,1)}, u32[]{:S(2)}, u32[]{:S(2)}) async-start(bf16[4,312,768]{2,1,0:T(8,128)(2,1)} %bitcast.332), calls=%async_computation.11 | async-start | bytes 3833856 | tf_op jit(solution)/shard_map/all_to_all | solution.py:391
  824.5 189.6 %all-to-all-start.9 = ((bf16[8,1248,768]{2,1,0:T(8,128)(2,1)}), bf16[8,1248,768]{2,1,0:T(8,128)(2,1)}, u32[]{:S(2)}, u32[]{:S(2)}) async-start(bf16[8,1248,768]{2,1,0:T(8,128)(2,1)} %bitcast.304), calls=%async_computation.9 | async-start | bytes 30670848 | tf_op jit(solution)/shard_map/all_to_all | solution.py:391
  830.2 262.9 %all-gather.40.cloned.1.call-start = ((), (), s32[]{:S(2)}) async-start(), calls=%async_computation.20 | async-start | bytes 1966080 | tf_op jit(solution)/shard_map/all_gather | solution.py:558
  831.0 297.4 %all-gather.42.cloned.1.call-start = ((), (), s32[]{:S(2)}) async-start(), calls=%async_computation.21 | async-start | bytes 1966080 | tf_op jit(solution)/shard_map/all_gather | solution.py:608
  835.3 296.4 %all-gather.50.cloned.1.call-start = ((), (), s32[]{:S(2)}) async-start(), calls=%async_computation.25 | async-start | bytes 4313088 | tf_op jit(solution)/shard_map/all_gather | solution.py:596
  838.1 301.0 %all-gather.48.cloned.1.call-start = ((), (), s32[]{:S(2)}) async-start(), calls=%async_computation.24 | async-start | bytes 4313088 | tf_op jit(solution)/shard_map/all_gather | solution.py:596
  (128 other events, 2057.6 us)
Sparse Core Ops, SparseCore 0:
  24.1 45.4 all-gather.43
  72.2 32.8 all-gather.23
  110.6 42.7 all-gather.45
  155.7 22.9 all-gather.25
  181.0 38.9 all-gather.27
  222.2 38.9 all-gather.29
  263.6 33.9 all-gather.31
  302.0 30.6 all-gather.33
  335.1 43.0 all-gather.35
  380.5 38.9 all-gather.37
  832.6 38.9 all-gather.39
  873.6 35.9 all-gather.41
  912.0 86.4 all-gather.49
  1073.9 35.5 all-gather.47
